TPU v7x, 32 devices: a whole 2x2x4 slice. The times are simulated.
32 devices in a mesh: rep: 4 (over z), fsdp: 8 (over y, x, core).
Axes of the slice: x: 2, y: 2, z: 4, core: 2. Of those that a mesh axis runs over, the one named last changes fastest.
Arguments:
- tokens: bfloat16 [64, 512, 768], P(('rep', 'fsdp')), may hold values from -6 to 6
- segment_ids: int32 [64, 512], P(('rep', 'fsdp')), may hold values from 0 to 7, never falling along the last dimension, each value on 1 to 128 neighbouring positions
- pairing: int32 [512], replicated, may hold values from 0 to 511, each once
- query_weight: bfloat16 [768, 768], P('fsdp'), may hold values from -0.21875 to 0.21875
- key_weight: bfloat16 [768, 768], P('fsdp'), may hold values from -0.21875 to 0.21875
- value_weight: bfloat16 [768, 768], P('fsdp'), may hold values from -0.21875 to 0.21875
- out_weight: bfloat16 [768, 768], P('fsdp'), may hold values from -0.625 to 0.625
- up_weight: bfloat16 [768, 3072], P('fsdp'), may hold values from -0.21875 to 0.21875
- down_weight: bfloat16 [3072, 768], P('fsdp'), may hold values from -0.109375 to 0.109375
- query_bias: bfloat16 [768], P('fsdp'), may hold values from -3 to 3
- value_bias: bfloat16 [768], P('fsdp'), may hold values from -3 to 3
- out_bias: bfloat16 [768], P('fsdp'), may hold values from -3 to 3
- up_bias: bfloat16 [3072], P('fsdp'), may hold values from -3 to 3
- down_bias: bfloat16 [768], P('fsdp'), may hold values from -3 to 3
- first_gain: bfloat16 [768], P('fsdp'), may hold values from 0.5 to 1.5
- first_shift: bfloat16 [768], P('fsdp'), may hold values from -1 to 1
- second_gain: bfloat16 [768], P('fsdp'), may hold values from 0.5 to 1.5
- second_shift: bfloat16 [768], P('fsdp'), may hold values from -0.5 to 0.5
Outputs:
- layer_output: bfloat16 [64, 512, 768], P(('rep', 'fsdp'))
- grad_tokens: bfloat16 [64, 512, 768], P(('rep', 'fsdp'))
- grad_query_weight: float32 [768, 768], P('fsdp')
- grad_key_weight: float32 [768, 768], P('fsdp')
- grad_value_weight: float32 [768, 768], P('fsdp')
- grad_out_weight: float32 [768, 768], P('fsdp')
- grad_up_weight: float32 [768, 3072], P('fsdp')
- grad_down_weight: float32 [3072, 768], P('fsdp')
- grad_query_bias: float32 [768], P('fsdp')
- grad_value_bias: float32 [768], P('fsdp')
- grad_out_bias: float32 [768], P('fsdp')
- grad_up_bias: float32 [3072], P('fsdp')
- grad_down_bias: float32 [768], P('fsdp')
- grad_first_gain: float32 [768], P('fsdp')
- grad_first_shift: float32 [768], P('fsdp')
- grad_second_gain: float32 [768], P('fsdp')
- grad_second_shift: float32 [768], P('fsdp')
Inputs may be any that keep to these rules, and one draw needn't show every extreme that they name: `segment_ids`: within each row the ids never fall, and each of 0 to 7 occurs on 1 to 128 positions. `pairing`: every text number occurs once.
All inputs are finite; a program needn't handle non-finite values.
Results may differ from a plain program's by a relative error of at most 0.015.
Values may be sent and summed in bfloat16 or wider, within the bound.
A program may use at most 192 MiB of HBM per device.

v0:
```python
import jax
import jax.numpy as jnp
from jax import lax
from jax.sharding import PartitionSpec as P

H = 12
HD = 64
SEGS = 8


def norm_piece(residual, gain_vector, shift_vector):
    centre = jnp.mean(residual, -1, keepdims=True)
    offset = residual - centre
    spread = jnp.mean(offset * offset, -1, keepdims=True)
    return offset * lax.rsqrt(spread + 1e-12) * gain_vector + shift_vector


def gelu_exact(argument):
    return jax.nn.gelu(argument, approximate=False)


def pool_texts(layer_out, segments):
    member = (segments[:, None] == jnp.arange(SEGS)[None, :]).astype(jnp.float32)
    totals = jnp.dot(member.T, layer_out, precision=lax.Precision.HIGHEST)
    counts = jnp.sum(member, 0)
    pooled = totals / counts[:, None]
    return pooled * lax.rsqrt(jnp.sum(pooled * pooled, -1, keepdims=True) + 1e-06)


def project(inputs, weight, bias_vector):
    return jnp.dot(inputs, weight, preferred_element_type=jnp.float32) + bias_vector.astype(
        jnp.float32
    )


def head_scores(query_states, key_states, segments):
    row_length = query_states.shape[0]
    scores = jnp.einsum(
        "qhd,khd->hqk",
        query_states.reshape(row_length, H, HD),
        key_states.reshape(row_length, H, HD),
        preferred_element_type=jnp.float32,
    ) * HD ** (-0.5)
    same_text = segments[:, None] == segments[None, :]
    return jnp.where(same_text[None], scores, -1e30)


def attend_forward(pieces):
    query_states, key_states, value_states, segments = pieces
    row_length = query_states.shape[0]
    scores = head_scores(query_states, key_states, segments)
    row_peak = jnp.max(scores, -1, keepdims=True)
    exponent = jnp.exp(scores - row_peak)
    row_total = jnp.sum(exponent, -1, keepdims=True)
    probability = (exponent / row_total).astype(jnp.bfloat16)
    mixture = jnp.einsum(
        "hqk,khd->qhd",
        probability,
        value_states.reshape(row_length, H, HD),
        preferred_element_type=jnp.float32,
    )
    return (mixture.reshape(row_length, H * HD).astype(jnp.bfloat16), row_peak + jnp.log(row_total))


def attend_backward(pieces):
    query_states, key_states, value_states, segments, grad_mixture, log_total = pieces
    row_length = query_states.shape[0]
    query_heads = query_states.reshape(row_length, H, HD)
    key_heads = key_states.reshape(row_length, H, HD)
    value_heads = value_states.reshape(row_length, H, HD)
    grad_heads = grad_mixture.reshape(row_length, H, HD)
    probability = jnp.exp(head_scores(query_states, key_states, segments) - log_total)
    grad_probability = jnp.einsum(
        "qhd,khd->hqk", grad_heads, value_heads, preferred_element_type=jnp.float32
    )
    grad_values = jnp.einsum(
        "hqk,qhd->khd",
        probability.astype(jnp.bfloat16),
        grad_heads,
        preferred_element_type=jnp.float32,
    )
    grad_scores = probability * (
        grad_probability - jnp.sum(probability * grad_probability, -1, keepdims=True)
    )
    grad_scores = grad_scores.astype(jnp.bfloat16)
    score_scale = HD ** (-0.5)
    grad_queries = (
        jnp.einsum("hqk,khd->qhd", grad_scores, key_heads, preferred_element_type=jnp.float32)
        * score_scale
    )
    grad_keys = (
        jnp.einsum("hqk,qhd->khd", grad_scores, query_heads, preferred_element_type=jnp.float32)
        * score_scale
    )
    return (
        grad_queries.reshape(row_length, H * HD).astype(jnp.bfloat16),
        grad_keys.reshape(row_length, H * HD).astype(jnp.bfloat16),
        grad_values.reshape(row_length, H * HD).astype(jnp.bfloat16),
    )


def run_layer(tokens, params, segment_ids):
    (
        query_weight,
        key_weight,
        value_weight,
        out_weight,
        up_weight,
        down_weight,
        query_bias,
        value_bias,
        out_bias,
        up_bias,
        down_bias,
        first_gain,
        first_shift,
        second_gain,
        second_shift,
    ) = params
    row_count, row_length, feature_width = tokens.shape
    flat_tokens = tokens.reshape(row_count * row_length, feature_width)
    query_states = project(flat_tokens, query_weight, query_bias).astype(jnp.bfloat16)
    key_states = jnp.dot(flat_tokens, key_weight, preferred_element_type=jnp.float32).astype(
        jnp.bfloat16
    )
    value_states = project(flat_tokens, value_weight, value_bias).astype(jnp.bfloat16)
    row_shape = (row_count, row_length, feature_width)
    joined, log_total = lax.map(
        attend_forward,
        (
            query_states.reshape(row_shape),
            key_states.reshape(row_shape),
            value_states.reshape(row_shape),
            segment_ids,
        ),
    )
    joined = joined.reshape(row_count * row_length, feature_width)
    resid_one = flat_tokens.astype(jnp.float32) + project(joined, out_weight, out_bias)
    hidden = norm_piece(resid_one, first_gain.astype(jnp.float32), first_shift.astype(jnp.float32))
    expanded = project(hidden.astype(jnp.bfloat16), up_weight, up_bias)
    active = gelu_exact(expanded).astype(jnp.bfloat16)
    resid_two = hidden + project(active, down_weight, down_bias)
    output = norm_piece(
        resid_two, second_gain.astype(jnp.float32), second_shift.astype(jnp.float32)
    )
    return (
        flat_tokens,
        query_states,
        key_states,
        value_states,
        joined,
        log_total,
        resid_one,
        hidden,
        expanded,
        active,
        resid_two,
        output,
    )


def local(
    tokens,
    segment_ids,
    pairing,
    query_weight,
    key_weight,
    value_weight,
    out_weight,
    up_weight,
    down_weight,
    query_bias,
    value_bias,
    out_bias,
    up_bias,
    down_bias,
    first_gain,
    first_shift,
    second_gain,
    second_shift,
):
    shards = (
        query_weight,
        key_weight,
        value_weight,
        out_weight,
        up_weight,
        down_weight,
        query_bias,
        value_bias,
        out_bias,
        up_bias,
        down_bias,
        first_gain,
        first_shift,
        second_gain,
        second_shift,
    )
    params = (
        lax.all_gather(shards[0], "fsdp", axis=0, tiled=True),
        lax.all_gather(shards[1], "fsdp", axis=0, tiled=True),
        lax.all_gather(shards[2], "fsdp", axis=0, tiled=True),
        lax.all_gather(shards[3], "fsdp", axis=0, tiled=True),
        lax.all_gather(shards[4], "fsdp", axis=0, tiled=True),
        lax.all_gather(shards[5], "fsdp", axis=0, tiled=True),
        lax.all_gather(shards[6], "fsdp", axis=0, tiled=True),
        lax.all_gather(shards[7], "fsdp", axis=0, tiled=True),
        lax.all_gather(shards[8], "fsdp", axis=0, tiled=True),
        lax.all_gather(shards[9], "fsdp", axis=0, tiled=True),
        lax.all_gather(shards[10], "fsdp", axis=0, tiled=True),
        lax.all_gather(shards[11], "fsdp", axis=0, tiled=True),
        lax.all_gather(shards[12], "fsdp", axis=0, tiled=True),
        lax.all_gather(shards[13], "fsdp", axis=0, tiled=True),
        lax.all_gather(shards[14], "fsdp", axis=0, tiled=True),
    )
    row_count, row_length, feature_width = tokens.shape
    states = run_layer(tokens, params, segment_ids)
    output = states[11].reshape(row_count, row_length, feature_width)

    def embed_rows(layer_out):
        return jax.vmap(pool_texts)(layer_out, segment_ids)

    embedded, embed_pullback = jax.vjp(embed_rows, output)
    local_count = row_count * SEGS
    local_embed = embedded.reshape(local_count, feature_width).astype(jnp.bfloat16)
    everything = lax.all_gather(local_embed, ("rep", "fsdp"), axis=0, tiled=True)
    text_count = everything.shape[0]
    pair_count = text_count // 2
    local_ids = lax.axis_index(("rep", "fsdp")) * local_count + jnp.arange(
        local_count, dtype=jnp.int32
    )
    matches = pairing[None, :] == local_ids[:, None]
    position = jnp.sum(jnp.where(matches, jnp.arange(text_count, dtype=jnp.int32)[None, :], 0), 1)
    pair_index = position // 2
    query_flag = position % 2 == 0
    passages = everything[pairing[1::2]]
    logits = (
        jnp.einsum("td,pd->tp", local_embed, passages, preferred_element_type=jnp.float32) * 100.0
    )
    row_peak = jnp.max(logits, 1, keepdims=True)
    exponent = jnp.exp(logits - row_peak)
    softmax_rows = exponent / jnp.sum(exponent, 1, keepdims=True)
    target = (jnp.arange(pair_count, dtype=jnp.int32)[None, :] == pair_index[:, None]).astype(
        jnp.float32
    )
    grad_logits = jnp.where(query_flag[:, None], softmax_rows - target, 0.0)
    scaled = (grad_logits * 100.0).astype(jnp.bfloat16)
    grad_query = jnp.einsum("tp,pd->td", scaled, passages, preferred_element_type=jnp.float32)
    grad_passage = jnp.einsum("tp,td->pd", scaled, local_embed, preferred_element_type=jnp.float32)
    text_terms = (
        jnp.zeros((text_count, feature_width), jnp.float32).at[pairing[1::2]].set(grad_passage)
    )
    received = lax.psum_scatter(text_terms, ("rep", "fsdp"), scatter_dimension=0, tiled=True)
    grad_embed = grad_query + received
    (grad_output,) = embed_pullback(grad_embed.reshape(row_count, SEGS, feature_width))
    params = (
        lax.all_gather(shards[0], "fsdp", axis=0, tiled=True),
        lax.all_gather(shards[1], "fsdp", axis=0, tiled=True),
        lax.all_gather(shards[2], "fsdp", axis=0, tiled=True),
        lax.all_gather(shards[3], "fsdp", axis=0, tiled=True),
        lax.all_gather(shards[4], "fsdp", axis=0, tiled=True),
        lax.all_gather(shards[5], "fsdp", axis=0, tiled=True),
        lax.all_gather(shards[6], "fsdp", axis=0, tiled=True),
        lax.all_gather(shards[7], "fsdp", axis=0, tiled=True),
        lax.all_gather(shards[8], "fsdp", axis=0, tiled=True),
        lax.all_gather(shards[9], "fsdp", axis=0, tiled=True),
        lax.all_gather(shards[10], "fsdp", axis=0, tiled=True),
        lax.all_gather(shards[11], "fsdp", axis=0, tiled=True),
        lax.all_gather(shards[12], "fsdp", axis=0, tiled=True),
        lax.all_gather(shards[13], "fsdp", axis=0, tiled=True),
        lax.all_gather(shards[14], "fsdp", axis=0, tiled=True),
    )
    states = run_layer(tokens, params, segment_ids)
    flat_tokens, query_states, key_states, value_states, joined, log_total = states[:6]
    resid_one, hidden, expanded, active, resid_two = states[6:11]
    w_query_full, w_key_full, w_value_full, w_out_full, w_up_full, w_down_full = params[:6]
    first_gain_f = params[11].astype(jnp.float32)
    first_shift_f = params[12].astype(jnp.float32)
    second_gain_f = params[13].astype(jnp.float32)
    second_shift_f = params[14].astype(jnp.float32)
    token_total = row_count * row_length
    norm_out, second_pullback = jax.vjp(norm_piece, resid_two, second_gain_f, second_shift_f)
    grad_resid_two, grad_second_gain, grad_second_shift = second_pullback(
        grad_output.reshape(token_total, feature_width)
    )
    grad_feed = grad_resid_two.astype(jnp.bfloat16)
    grad_down_weight = jnp.einsum(
        "nf,nd->fd", active, grad_feed, preferred_element_type=jnp.float32
    )
    grad_down_bias = jnp.sum(grad_feed.astype(jnp.float32), 0)
    grad_active = jnp.einsum(
        "nd,fd->nf", grad_feed, w_down_full, preferred_element_type=jnp.float32
    )
    gelu_out, gelu_pullback = jax.vjp(gelu_exact, expanded)
    grad_expanded = gelu_pullback(grad_active)[0].astype(jnp.bfloat16)
    grad_up_weight = jnp.einsum(
        "nd,nf->df", hidden.astype(jnp.bfloat16), grad_expanded, preferred_element_type=jnp.float32
    )
    grad_up_bias = jnp.sum(grad_expanded.astype(jnp.float32), 0)
    grad_hidden = grad_resid_two + jnp.einsum(
        "nf,df->nd", grad_expanded, w_up_full, preferred_element_type=jnp.float32
    )
    hidden_out, first_pullback = jax.vjp(norm_piece, resid_one, first_gain_f, first_shift_f)
    grad_resid_one, grad_first_gain, grad_first_shift = first_pullback(grad_hidden)
    grad_branch = grad_resid_one.astype(jnp.bfloat16)
    grad_out_weight = jnp.einsum(
        "nd,ne->de", joined, grad_branch, preferred_element_type=jnp.float32
    )
    grad_out_bias = jnp.sum(grad_branch.astype(jnp.float32), 0)
    grad_joined = jnp.einsum(
        "ne,de->nd", grad_branch, w_out_full, preferred_element_type=jnp.float32
    ).astype(jnp.bfloat16)
    row_shape = (row_count, row_length, feature_width)
    grad_queries, grad_keys, grad_values = lax.map(
        attend_backward,
        (
            query_states.reshape(row_shape),
            key_states.reshape(row_shape),
            value_states.reshape(row_shape),
            segment_ids,
            grad_joined.reshape(row_shape),
            log_total,
        ),
    )
    grad_queries = grad_queries.reshape(token_total, feature_width)
    grad_keys = grad_keys.reshape(token_total, feature_width)
    grad_values = grad_values.reshape(token_total, feature_width)
    grad_query_weight = jnp.einsum(
        "nd,ne->de", flat_tokens, grad_queries, preferred_element_type=jnp.float32
    )
    grad_key_weight = jnp.einsum(
        "nd,ne->de", flat_tokens, grad_keys, preferred_element_type=jnp.float32
    )
    grad_value_weight = jnp.einsum(
        "nd,ne->de", flat_tokens, grad_values, preferred_element_type=jnp.float32
    )
    grad_query_bias = jnp.sum(grad_queries.astype(jnp.float32), 0)
    grad_value_bias = jnp.sum(grad_values.astype(jnp.float32), 0)
    grad_inputs = grad_resid_one
    grad_inputs = grad_inputs + jnp.einsum(
        "ne,de->nd", grad_queries, w_query_full, preferred_element_type=jnp.float32
    )
    grad_inputs = grad_inputs + jnp.einsum(
        "ne,de->nd", grad_keys, w_key_full, preferred_element_type=jnp.float32
    )
    grad_inputs = grad_inputs + jnp.einsum(
        "ne,de->nd", grad_values, w_value_full, preferred_element_type=jnp.float32
    )
    grad_params = (
        grad_query_weight,
        grad_key_weight,
        grad_value_weight,
        grad_out_weight,
        grad_up_weight,
        grad_down_weight,
        grad_query_bias,
        grad_value_bias,
        grad_out_bias,
        grad_up_bias,
        grad_down_bias,
        grad_first_gain,
        grad_first_shift,
        grad_second_gain,
        grad_second_shift,
    )
    shares = (
        lax.psum_scatter(grad_params[0], "fsdp", scatter_dimension=0, tiled=True),
        lax.psum_scatter(grad_params[1], "fsdp", scatter_dimension=0, tiled=True),
        lax.psum_scatter(grad_params[2], "fsdp", scatter_dimension=0, tiled=True),
        lax.psum_scatter(grad_params[3], "fsdp", scatter_dimension=0, tiled=True),
        lax.psum_scatter(grad_params[4], "fsdp", scatter_dimension=0, tiled=True),
        lax.psum_scatter(grad_params[5], "fsdp", scatter_dimension=0, tiled=True),
        lax.psum_scatter(grad_params[6], "fsdp", scatter_dimension=0, tiled=True),
        lax.psum_scatter(grad_params[7], "fsdp", scatter_dimension=0, tiled=True),
        lax.psum_scatter(grad_params[8], "fsdp", scatter_dimension=0, tiled=True),
        lax.psum_scatter(grad_params[9], "fsdp", scatter_dimension=0, tiled=True),
        lax.psum_scatter(grad_params[10], "fsdp", scatter_dimension=0, tiled=True),
        lax.psum_scatter(grad_params[11], "fsdp", scatter_dimension=0, tiled=True),
        lax.psum_scatter(grad_params[12], "fsdp", scatter_dimension=0, tiled=True),
        lax.psum_scatter(grad_params[13], "fsdp", scatter_dimension=0, tiled=True),
        lax.psum_scatter(grad_params[14], "fsdp", scatter_dimension=0, tiled=True),
    )
    totals = (
        lax.psum(shares[0].astype(jnp.bfloat16), "rep").astype(jnp.float32),
        lax.psum(shares[1].astype(jnp.bfloat16), "rep").astype(jnp.float32),
        lax.psum(shares[2].astype(jnp.bfloat16), "rep").astype(jnp.float32),
        lax.psum(shares[3].astype(jnp.bfloat16), "rep").astype(jnp.float32),
        lax.psum(shares[4].astype(jnp.bfloat16), "rep").astype(jnp.float32),
        lax.psum(shares[5].astype(jnp.bfloat16), "rep").astype(jnp.float32),
        lax.psum(shares[6].astype(jnp.bfloat16), "rep").astype(jnp.float32),
        lax.psum(shares[7].astype(jnp.bfloat16), "rep").astype(jnp.float32),
        lax.psum(shares[8].astype(jnp.bfloat16), "rep").astype(jnp.float32),
        lax.psum(shares[9].astype(jnp.bfloat16), "rep").astype(jnp.float32),
        lax.psum(shares[10].astype(jnp.bfloat16), "rep").astype(jnp.float32),
        lax.psum(shares[11].astype(jnp.bfloat16), "rep").astype(jnp.float32),
        lax.psum(shares[12].astype(jnp.bfloat16), "rep").astype(jnp.float32),
        lax.psum(shares[13].astype(jnp.bfloat16), "rep").astype(jnp.float32),
        lax.psum(shares[14].astype(jnp.bfloat16), "rep").astype(jnp.float32),
    )
    return (
        output.astype(jnp.bfloat16),
        grad_inputs.reshape(row_shape).astype(jnp.bfloat16),
    ) + tuple(totals)


def solution(mesh):
    in_specs = (
        P(("rep", "fsdp"), None, None),
        P(("rep", "fsdp"), None),
        P(),
        P("fsdp", None),
        P("fsdp", None),
        P("fsdp", None),
        P("fsdp", None),
        P("fsdp", None),
        P("fsdp", None),
        P("fsdp"),
        P("fsdp"),
        P("fsdp"),
        P("fsdp"),
        P("fsdp"),
        P("fsdp"),
        P("fsdp"),
        P("fsdp"),
        P("fsdp"),
    )
    out_specs = (
        P(("rep", "fsdp"), None, None),
        P(("rep", "fsdp"), None, None),
        P("fsdp", None),
        P("fsdp", None),
        P("fsdp", None),
        P("fsdp", None),
        P("fsdp", None),
        P("fsdp", None),
        P("fsdp"),
        P("fsdp"),
        P("fsdp"),
        P("fsdp"),
        P("fsdp"),
        P("fsdp"),
        P("fsdp"),
        P("fsdp"),
        P("fsdp"),
    )
    return jax.shard_map(local, mesh=mesh, in_specs=in_specs, out_specs=out_specs, check_vma=False)
```

profile of v0, /device:TPU:0, one launch (start us, length us, event | category | flops | bytes accessed | tf_op | source)
XLA Modules:
  0.0 919.3 jit_solution(18357298605444102723)
XLA Ops:
  24.8 25.7 %all-reduce.18 = (bf16[768]{0:T(1024)(128)(2,1)S(1)}, bf16[768]{0:T(1024)(128)(2,1)S(1)}, bf16[768]{0:T(1024)(128)(2,1)S(1)}, bf16[768]{0:T(1024)(128)(2,1)S(1)}...) all-reduce(bf16[768]{0:T(1024)(128)(2,1)S(1)} %dynamic-update-slice, ...), channel_id=1, replica_groups=mesh['rep'=4,'fsdp'=8] {'fsdp'}, use_global_device_ids=true, to_apply=%add.1 | all-reduce | flops 6144 | bytes 24576
  73.1 15.7 %all-gather.12.cloned.1.call-done = bf16[768,768]{1,0:T(8,128)(2,1)} async-done(((bf16[96,768]{1,0:T(8,128)(2,1)}), bf16[768,768]{1,0:T(8,128)(2,1)}) %all-gather.12.cloned.1.call-update) | async-done | bytes 1179664 | tf_op jit(solution)/shard_map/all_gather | solution.py:201
  96.9 51.6 %while.36 = (s32[]{:T(128)}, bf16[2,512,768]{2,1,0:T(8,128)(2,1)}, bf16[2,512,768]{1,2,0:T(8,128)(2,1)S(1)}, s32[2,512]{1,0:T(2,128)S(1)}, bf16[2,512,768]{1,2,0...) while((s32[]{:T(128)}, bf16[2,512,768]{2,1,0:T(8,128)(2,1)}, bf16[2,512,768]{1,2,0:T(8,128)(2,1)S(1)}, ...), condition=%wide.region_3.4_spmd, body=%wide.region_0.3_spmd.sunk | while | flops 824836608 | bytes 36755556 | solution.py:128
  100.5 10.5 %fusion.226 = (f32[12,512]{1,0:T(8,128)S(1)}, f32[12,512,512]{1,2,0:T(8,128)}) fusion(pred[512,512]{0,1:T(8,128)(4,1)S(1)} %broadcast_compare_fusion.6, bf16[512,12,64]{0,2,1:T(8,128)(2,1)} %bitcast.230, bf16[512,12,64]{0,2,1:T(8,128)(2,1)} %bitcast.229), kind=kOutput, calls=%fused_computation.233.clone.1 | convolution fusion | flops 415236608 | bytes 14442496 | tf_op jit(solution)/shard_map/while/body/eval_jaxpr/sub | solution.py:53
  126.0 10.5 %fusion.226 = (f32[12,512]{1,0:T(8,128)S(1)}, f32[12,512,512]{1,2,0:T(8,128)}) fusion(pred[512,512]{0,1:T(8,128)(4,1)S(1)} %broadcast_compare_fusion.6, bf16[512,12,64]{0,2,1:T(8,128)(2,1)} %bitcast.230, bf16[512,12,64]{0,2,1:T(8,128)(2,1)} %bitcast.229), kind=kOutput, calls=%fused_computation.233.clone.1 | convolution fusion | flops 415236608 | bytes 14442496 | tf_op jit(solution)/shard_map/while/body/eval_jaxpr/sub | solution.py:53
  149.8 34.3 %while.37 = (s32[]{:T(128)}, bf16[2,512,768]{2,1,0:T(8,128)(2,1)}, f32[2,12,512,1]{2,1,3,0:T(8,128)S(1)}, bf16[2,512,768]{1,2,0:T(8,128)(2,1)S(1)}, s32[2,512]{1...) while((s32[]{:T(128)}, bf16[2,512,768]{2,1,0:T(8,128)(2,1)}, ...), condition=%wide.region_19.20_spmd, body=%wide.region_16.19_spmd.sunk | while | flops 843704320 | bytes 50034800 | solution.py:128
  196.8 36.5 %fusion.50.clone.4 = bf16[1024,3072]{1,0:T(8,128)(2,1)} fusion(f32[3072]{0:T(1024)S(1)} %bitcast.247, bf16[768,3072]{1,0:T(8,128)(2,1)} %all-gather.16.cloned.1.call-done, f32[1024,768]{1,0:T(8,128)S(1)} %copy-done.26, f32[768]{0:T(1024)S(1)} %copy-done.54, f32[768]{0:T(1024)S(1)} %copy-done.49, ...), kind=kOutput, calls=%fused_computation.62.clone.clone.clone.clone.clone.clone.1 | convolution fusion | flops 5043388416 | bytes 14182400 | tf_op jit(solution)/shard_map/dot_general | solution.py:31
  233.4 9.0 fusion.120
  246.5 45.2 %all_gather.77 = bf16[512,768]{1,0:T(8,128)(2,1)} all-gather(bf16[16,768]{1,0:T(8,128)(2,1)S(1)} %fusion.69), channel_id=1, replica_groups=mesh['rep'=4,'fsdp'=8] {'rep','fsdp'}, dimensions={0}, use_global_device_ids=true | all-gather | bytes 811008 | tf_op jit(solution)/shard_map/all_gather | solution.py:226
  302.3 37.7 %multiply_convert_fusion.3 = (bf16[1024,3072]{1,0:T(8,128)(2,1)S(1)}, f32[1024,3072]{1,0:T(8,128)}, f32[1024,3072]{1,0:T(8,128)}) fusion(f32[3072]{0:T(1024)} %bitcast.246, bf16[768,3072]{1,0:T(8,128)(2,1)} %all-gather.16.cloned.1.call-done, f32[1024,768]{1,0:T(8,128)S(1)} %copy-done.7, f32[1024]{0:T(1024)S(1)} %copy-done.46, f32[1024]{0:T(1024)S(1)} %copy-done.44, ...), kind=kOutput, calls=%fused_computation.66 | convolution fusion | flops 5043388416 | bytes 39348224 | tf_op jit(solution)/shard_map/dot_general | solution.py:31
  340.0 10.0 %fusion.125 = (f32[1024]{0:T(1024)S(1)}, f32[1024,768]{1,0:T(8,128)S(1)}) fusion(f32[768]{0:T(1024)S(1)} %copy-done.86, bf16[1024,3072]{1,0:T(8,128)(2,1)S(1)} %get-tuple-element.398, bf16[3072,768]{1,0:T(8,128)(2,1)} %all-gather.18.cloned.1.call-done, f32[768]{0:T(1024)S(1)} %copy-done.55, f32[768]{0:T(1024)S(1)} %copy-done.49, f32[1024]{0:T(1024)S(1)} %copy-done.46, ...), kind=kOutput, calls=%fused_computation.239 | convolution fusion | flops 4837342208 | bytes 17323008 | tf_op jit(solution)/shard_map/dot_general | solution.py:31
  353.3 42.2 %reduce-scatter.14.cloned.1.call-done = f32[16,768]{1,0:T(8,128)} async-done(((f32[512,768]{1,0:T(8,128)}), f32[16,768]{1,0:T(8,128)}) %reduce-scatter.14.cloned.1.call-update) | async-done | bytes 49168 | tf_op jit(solution)/shard_map/reduce_scatter | solution.py:253
  405.7 18.7 %convert_reduce_fusion = (f32[3072]{0:T(1024)}, bf16[1024,3072]{1,0:T(8,128)(2,1)}) fusion(f32[1024,3072]{1,0:T(8,128)} %get-tuple-element.399, bf16[1024,768]{1,0:T(8,128)(2,1)} %get-tuple-element.391, bf16[3072,768]{1,0:T(8,128)(2,1)} %all-gather.18.cloned.1.call-done, f32[1024,3072]{1,0:T(8,128)} %get-tuple-element.426, f32[3072]{0:T(1024)S(1)} %bitcast.248), kind=kOutput, calls=%fused_computation.64 | convolution fusion | flops 4885312512 | bytes 37773312 | tf_op jit(solution)/shard_map/nd,fd->nf/dot_general | solution.py:291
  424.5 10.3 %multiply_reduce_fusion.1 = (f32[768]{0:T(1024)}, f32[1024]{0:T(1024)S(1)}, f32[768]{0:T(1024)}, f32[1024,768]{1,0:T(8,128)S(1)}) fusion(f32[1024,768]{1,0:T(8,128)S(1)} %copy-done.7, f32[1024]{0:T(1024)S(1)} %copy-done.46, f32[1024]{0:T(1024)S(1)} %copy-done.44, f32[768]{0:T(1024)S(1)} %copy-done.49, bf16[1024,3072]{1,0:T(8,128)(2,1)} %get-tuple-element.431, ...), kind=kOutput, calls=%fused_computation.104 | convolution fusion | flops 4839699456 | bytes 20472832 | tf_op jit(solution)/shard_map/nf,df->nd/dot_general | solution.py:300
  447.5 66.9 %while.38 = (s32[]{:T(128)}, bf16[2,512,768]{1,2,0:T(8,128)(2,1)}, bf16[2,512,768]{1,2,0:T(8,128)(2,1)}, bf16[2,512,768]{1,2,0:T(8,128)(2,1)}, bf16[2,512,768]{1...) while((s32[]{:T(128)}, bf16[2,512,768]{1,2,0:T(8,128)(2,1)}, ...), condition=%wide.region_30.31_spmd, body=%wide.region_28.30_spmd.sunk | while | flops 2062673920 | bytes 163232176 | solution.py:314
  535.0 10.7 %fusion.110 = f32[768,3072]{1,0:T(8,128)} fusion(bf16[1024,3072]{1,0:T(8,128)(2,1)} %get-tuple-element.431, f32[1024,768]{1,0:T(8,128)S(1)} %copy-done.8, f32[1024]{0:T(1024)S(1)} %copy-done.47, f32[1024]{0:T(1024)S(1)} %copy-done.45, f32[768]{0:T(1024)S(1)} %copy-done.56, f32[768]{0:T(1024)S(1)} %copy-done.50), kind=kOutput, calls=%fused_computation.229 | convolution fusion | flops 4835770368 | bytes 18888704 | tf_op jit(solution)/shard_map/nd,nf->df/dot_general | solution.py:296
  547.1 10.3 %fusion.131 = f32[3072,768]{1,0:T(8,128)} fusion(bf16[1024,3072]{1,0:T(8,128)(2,1)} %copy-done.94, bf16[1024,768]{1,0:T(8,128)(2,1)S(1)} %copy-done.32), kind=kOutput, calls=%fused_computation.246 | convolution fusion | flops 4831838208 | bytes 17301504 | tf_op jit(solution)/shard_map/nf,nd->fd/dot_general | solution.py:287
  570.3 39.2 %reduce-scatter.26.cloned.1.call-done = f32[96,768]{1,0:T(8,128)} async-done(((f32[768,768]{1,0:T(8,128)}), f32[96,768]{1,0:T(8,128)}) %reduce-scatter.26.cloned.1.call-update) | async-done | bytes 294928
  611.3 44.5 %reduce-scatter.22.cloned.1.call-done = f32[96,768]{1,0:T(8,128)} async-done(((f32[768,768]{1,0:T(8,128)}), f32[96,768]{1,0:T(8,128)}) %reduce-scatter.22.cloned.1.call-update) | async-done | bytes 294928
  657.5 78.1 %reduce-scatter.18.cloned.1.call-done = f32[96,3072]{1,0:T(8,128)} async-done(((f32[768,3072]{1,0:T(8,128)}), f32[96,3072]{1,0:T(8,128)}) %reduce-scatter.18.cloned.1.call-update) | async-done | bytes 1179664 | tf_op jit(solution)/shard_map/reduce_scatter | solution.py:371
  737.8 77.8 %reduce-scatter.20.cloned.1.call-done = f32[384,768]{1,0:T(8,128)} async-done(((f32[3072,768]{1,0:T(8,128)}), f32[384,768]{1,0:T(8,128)}) %reduce-scatter.20.cloned.1.call-update) | async-done | bytes 1179664 | tf_op jit(solution)/shard_map/reduce_scatter | solution.py:372
  818.4 24.8 %all-reduce.17 = (bf16[768]{0:T(1024)(128)(2,1)S(1)}, bf16[768]{0:T(1024)(128)(2,1)S(1)}, bf16[768]{0:T(1024)(128)(2,1)S(1)}, bf16[3072]{0:T(1024)(128)(2,1)S(1)...) all-reduce(f32[768]{0:T(1024)S(1)} %get-tuple-element.435, ...), channel_id=9, replica_groups=mesh['rep'=4,'fsdp'=8] {'fsdp'}, use_global_device_ids=true, to_apply=%region_44.45.clone | all-reduce | flops 9216 | bytes 55296
  843.8 13.1 %all-reduce.19 = (bf16[96]{0:T(256)(128)(2,1)S(1)}, bf16[96]{0:T(256)(128)(2,1)S(1)}, bf16[96]{0:T(256)(128)(2,1)S(1)}, bf16[384]{0:T(512)(128)(2,1)S(1)}, bf16[...) all-reduce(bf16[96]{0:T(256)(128)(2,1)S(1)} %dynamic-slice.43, ...), channel_id=1, replica_groups=mesh['rep'=4,'fsdp'=8] {'rep'}, use_global_device_ids=true, to_apply=%region_45.46 | all-reduce | flops 1152 | bytes 4608 | tf_op jit(solution)/shard_map/psum | solution.py:390
  870.6 31.6 %all-reduce.23.cloned.1.call-done = (bf16[96,768]{0,1:T(8,128)(2,1)}, bf16[96,768]{0,1:T(8,128)(2,1)}, bf16[96,768]{0,1:T(8,128)(2,1)}, bf16[96,768]{1,0:T(8,128...) async-done(((bf16[96,768]{0,1:T(8,128)(2,1)}, bf16[96,768]{0,1:T(8,128)(2,1)}, bf16[96,768]{0,1:T(8,128)(2,1)}, bf16[96,768]{1,0:T(8,128)(2,1)}, ...) | async-done | bytes 1769488 | tf_op jit(solution)/shard_map/psum | solution.py:384
  (438 shorter events, 299.4 us)
Async XLA Ops:
  7.2 56.0 %all-gather.8.cloned.1.call-start = ((), (), s32[]{:S(2)}) async-start(), calls=%async_computation.7 | async-start | bytes 1327104 | tf_op jit(solution)/shard_map/all_gather | solution.py:202
  7.9 59.2 %all-gather.10.cloned.1.call-start = ((), (), s32[]{:S(2)}) async-start(), calls=%async_computation.8 | async-start | bytes 1327104 | tf_op jit(solution)/shard_map/all_gather | solution.py:200
  8.7 80.2 %all-gather.12.cloned.1.call-start = ((), (), s32[]{:S(2)}) async-start(), calls=%async_computation.9 | async-start | bytes 1327104 | tf_op jit(solution)/shard_map/all_gather | solution.py:201
  9.4 174.8 %all-gather.14.cloned.1.call-start = ((), (), s32[]{:S(2)}) async-start(), calls=%async_computation.10 | async-start | bytes 1327104 | tf_op jit(solution)/shard_map/all_gather | solution.py:203
  10.0 186.6 %all-gather.16.cloned.1.call-start = ((), (), s32[]{:S(2)}) async-start(), calls=%async_computation.11 | async-start | bytes 5308416 | tf_op jit(solution)/shard_map/all_gather | solution.py:204
  10.6 222.8 %all-gather.18.cloned.1.call-start = ((), (), s32[]{:S(2)}) async-start(), calls=%async_computation.12 | async-start | bytes 5308416 | tf_op jit(solution)/shard_map/all_gather | solution.py:205
  11.1 384.4 %reduce-scatter.14.cloned.1.call-start = ((), (), s32[]{:S(2)}) async-start(), calls=%async_computation.13 | async-start | bytes 1622016 | tf_op jit(solution)/shard_map/reduce_scatter | solution.py:253
  15.4 51.0 %copy-start.84 = (s32[256]{0:T(256)}, s32[256]{0:T(256)S(1)}, u32[]{:S(2)}) copy-start(s32[256]{0:T(256)S(1)} %compare_select_fusion) | copy-start | bytes 3076
  302.2 264.7 %reduce-scatter.16.cloned.1.call-start = ((), (), s32[]{:S(2)}) async-start(), calls=%async_computation.14 | async-start | bytes 2654208 | tf_op jit(solution)/shard_map/reduce_scatter | solution.py:370
  302.3 37.7 %copy-start.55 = (f32[768]{0:T(1024)S(1)}, f32[768]{0:T(1024)}, u32[]{:S(2)}) copy-start(f32[768]{0:T(1024)} %convert_element_type.308) | copy-start | bytes 9220
  302.3 37.7 %copy-start.86 = (f32[768]{0:T(1024)S(1)}, f32[768]{0:T(1024)}, u32[]{:S(2)}) copy-start(f32[768]{0:T(1024)} %convert_element_type.312) | copy-start | bytes 9220
  443.0 125.6 %reduce-scatter.24.cloned.1.call-start = ((), (), s32[]{:S(2)}) async-start(), calls=%async_computation.18 | async-start | bytes 2654208
  522.3 87.2 %reduce-scatter.26.cloned.1.call-start = ((), (), s32[]{:S(2)}) async-start(), calls=%async_computation.19 | async-start | bytes 2654208
  528.5 127.3 %reduce-scatter.22.cloned.1.call-start = ((), (), s32[]{:S(2)}) async-start(), calls=%async_computation.17 | async-start | bytes 2654208
  534.9 200.7 %reduce-scatter.18.cloned.1.call-start = ((), (), s32[]{:S(2)}) async-start(), calls=%async_computation.15 | async-start | bytes 10616832 | tf_op jit(solution)/shard_map/reduce_scatter | solution.py:371
  545.7 269.9 %reduce-scatter.20.cloned.1.call-start = ((), (), s32[]{:S(2)}) async-start(), calls=%async_computation.16 | async-start | bytes 10616832 | tf_op jit(solution)/shard_map/reduce_scatter | solution.py:372
  557.4 344.8 %all-reduce.23.cloned.1.call-start = ((), (), s32[]{:S(2)}) async-start(), calls=%async_computation.20 | async-start | bytes 3833856 | tf_op jit(solution)/shard_map/psum | solution.py:384
  737.8 80.5 %copy-start.72 = (f32[768]{0:T(1024)S(1)}, f32[768]{0:T(1024)}, u32[]{:S(2)}) copy-start(f32[768]{0:T(1024)} %get-tuple-element.432) | copy-start | bytes 9220
  737.8 80.5 %copy-start.73 = (f32[768]{0:T(1024)S(1)}, f32[768]{0:T(1024)}, u32[]{:S(2)}) copy-start(f32[768]{0:T(1024)} %get-tuple-element.390) | copy-start | bytes 9220
  737.8 80.6 %copy-start.74 = (f32[768]{0:T(1024)S(1)}, f32[768]{0:T(1024)}, u32[]{:S(2)}) copy-start(f32[768]{0:T(1024)} %get-tuple-element.392) | copy-start | bytes 9220
  737.8 80.6 %copy-start.75 = (f32[768]{0:T(1024)S(1)}, f32[768]{0:T(1024)}, u32[]{:S(2)}) copy-start(f32[768]{0:T(1024)} %get-tuple-element.307) | copy-start | bytes 9220
  737.8 80.6 %copy-start.78 = (f32[3072]{0:T(1024)S(1)}, f32[3072]{0:T(1024)}, u32[]{:S(2)}) copy-start(f32[3072]{0:T(1024)} %get-tuple-element.430) | copy-start | bytes 36868
  737.8 80.6 %copy-start.88 = (f32[768]{0:T(1024)S(1)}, f32[768]{0:T(1024)}, u32[]{:S(2)}) copy-start(f32[768]{0:T(1024)} %get-tuple-element.309) | copy-start | bytes 9220
  737.8 80.6 %copy-start.89 = (f32[768]{0:T(1024)S(1)}, f32[768]{0:T(1024)}, u32[]{:S(2)}) copy-start(f32[768]{0:T(1024)} %get-tuple-element.311) | copy-start | bytes 9220
  (94 other events, 383.7 us)
Sparse Core Ops, SparseCore 0:
  9.9 26.9 all-gather.7
  38.7 24.0 all-gather.9
  64.7 24.0 all-gather.11
  90.6 24.0 all-gather.13
  116.4 38.9 all-gather.15
  157.1 38.9 all-gather.17
  302.3 93.1 reduce-scatter.13
  443.0 41.5 reduce-scatter.15
  522.4 41.3 reduce-scatter.23
  567.0 42.4 reduce-scatter.25
  613.2 42.4 reduce-scatter.21
  659.1 76.4 reduce-scatter.17
  739.1 76.4 reduce-scatter.19
  818.9 83.2 all-reduce.22
where the time goes:
time: 924 us; the launch traced here: 919 us
  waiting for transfers between devices  333 us (36%)
  matrix products  277 us (30%)
  blocking collectives  117 us (13%)
  local copies, waits for them, and re-layouts  115 us (12%)
  other arithmetic  58.7 us (6%)
  between operations  17.3 us (2%)
    dot_general x8, matrix products, project(): jnp.dot(inputs, weight, preferred_element_type=jnp.float32)  107 us
    unnamed x17, waiting for transfers between devices  87.4 us
    reduce_scatter x1, waiting for transfers between devices, local(): lax.psum_scatter(grad_params[4], 'fsdp', scatter_dimension=0, tiled=True)  78.1 us
    reduce_scatter x1, waiting for transfers between devices, local(): lax.psum_scatter(grad_params[5], 'fsdp', scatter_dimension=0, tiled=True)  77.8 us
    unnamed x2, blocking collectives  50.5 us
    all_gather x1, blocking collectives, local(): lax.all_gather(local_embed, ('rep', 'fsdp'), axis=0, tiled=True)  45.2 us
    unnamed x208, local copies, waits for them, and re-layouts  45.1 us
    reduce_scatter x1, waiting for transfers between devices, local(): lax.psum_scatter(text_terms, ('rep', 'fsdp'), scatter_dimension=0, tiled=...  42.2 us
  transfers between devices with their start and end apart: 14, of which 7 were waited for; matrix products, arithmetic and copies ran while one was open for 38% of the time, Pallas kernels for 0%

commit v1 on v0

--- a/solution.py
+++ b/solution.py
@@ -157,6 +157,34 @@
         resid_two,
         output,
     )
+
+
+def gather_all(shards):
+    packed = jnp.concatenate([piece.reshape(-1) for piece in shards])
+    gathered = lax.all_gather(packed, "fsdp", axis=0, tiled=True)
+    gathered = gathered.reshape(-1, packed.size)
+    params, at = [], 0
+    for piece in shards:
+        part = gathered[:, at : at + piece.size]
+        params.append(part.reshape((-1,) + piece.shape[1:]))
+        at += piece.size
+    return tuple(params)
+
+
+def reduce_all(grad_params):
+    group = lax.axis_size("fsdp")
+    packed = jnp.concatenate(
+        [piece.astype(jnp.bfloat16).reshape(group, -1) for piece in grad_params], 1
+    )
+    share = lax.psum_scatter(packed.reshape(-1), "fsdp", scatter_dimension=0, tiled=True)
+    total = lax.psum(share, "rep").astype(jnp.float32)
+    totals, at = [], 0
+    for piece in grad_params:
+        count = piece.size // group
+        shape = (piece.shape[0] // group,) + piece.shape[1:]
+        totals.append(total[at : at + count].reshape(shape))
+        at += count
+    return tuple(totals)
 
 
 def local(
@@ -196,23 +224,7 @@
         second_gain,
         second_shift,
     )
-    params = (
-        lax.all_gather(shards[0], "fsdp", axis=0, tiled=True),
-        lax.all_gather(shards[1], "fsdp", axis=0, tiled=True),
-        lax.all_gather(shards[2], "fsdp", axis=0, tiled=True),
-        lax.all_gather(shards[3], "fsdp", axis=0, tiled=True),
-        lax.all_gather(shards[4], "fsdp", axis=0, tiled=True),
-        lax.all_gather(shards[5], "fsdp", axis=0, tiled=True),
-        lax.all_gather(shards[6], "fsdp", axis=0, tiled=True),
-        lax.all_gather(shards[7], "fsdp", axis=0, tiled=True),
-        lax.all_gather(shards[8], "fsdp", axis=0, tiled=True),
-        lax.all_gather(shards[9], "fsdp", axis=0, tiled=True),
-        lax.all_gather(shards[10], "fsdp", axis=0, tiled=True),
-        lax.all_gather(shards[11], "fsdp", axis=0, tiled=True),
-        lax.all_gather(shards[12], "fsdp", axis=0, tiled=True),
-        lax.all_gather(shards[13], "fsdp", axis=0, tiled=True),
-        lax.all_gather(shards[14], "fsdp", axis=0, tiled=True),
-    )
+    params = gather_all(shards)
     row_count, row_length, feature_width = tokens.shape
     states = run_layer(tokens, params, segment_ids)
     output = states[11].reshape(row_count, row_length, feature_width)
@@ -240,37 +252,22 @@
     row_peak = jnp.max(logits, 1, keepdims=True)
     exponent = jnp.exp(logits - row_peak)
     softmax_rows = exponent / jnp.sum(exponent, 1, keepdims=True)
-    target = (jnp.arange(pair_count, dtype=jnp.int32)[None, :] == pair_index[:, None]).astype(
-        jnp.float32
-    )
-    grad_logits = jnp.where(query_flag[:, None], softmax_rows - target, 0.0)
-    scaled = (grad_logits * 100.0).astype(jnp.bfloat16)
-    grad_query = jnp.einsum("tp,pd->td", scaled, passages, preferred_element_type=jnp.float32)
-    grad_passage = jnp.einsum("tp,td->pd", scaled, local_embed, preferred_element_type=jnp.float32)
-    text_terms = (
-        jnp.zeros((text_count, feature_width), jnp.float32).at[pairing[1::2]].set(grad_passage)
-    )
-    received = lax.psum_scatter(text_terms, ("rep", "fsdp"), scatter_dimension=0, tiled=True)
-    grad_embed = grad_query + received
+    pairs = jnp.arange(pair_count, dtype=jnp.int32)[None, :]
+    target = (pairs == pair_index[:, None]).astype(jnp.float32)
+    queries = everything[pairing[0::2]]
+    whole = jnp.einsum("qd,pd->qp", queries, passages, preferred_element_type=jnp.float32) * 100.0
+    peak_all = jnp.max(whole, 1)
+    total_all = jnp.sum(jnp.exp(whole - peak_all[:, None]), 1)
+    cross = jnp.einsum("td,qd->tq", local_embed, queries, preferred_element_type=jnp.float32) * 100.0
+    softmax_columns = jnp.exp(cross - peak_all[None, :]) / total_all[None, :]
+    scaled_rows = ((softmax_rows - target) * 100.0).astype(jnp.bfloat16)
+    scaled_columns = ((softmax_columns - target) * 100.0).astype(jnp.bfloat16)
+    grad_query = jnp.einsum("tp,pd->td", scaled_rows, passages, preferred_element_type=jnp.float32)
+    grad_passage = jnp.einsum(
+        "tq,qd->td", scaled_columns, queries, preferred_element_type=jnp.float32
+    )
+    grad_embed = jnp.where(query_flag[:, None], grad_query, grad_passage)
     (grad_output,) = embed_pullback(grad_embed.reshape(row_count, SEGS, feature_width))
-    params = (
-        lax.all_gather(shards[0], "fsdp", axis=0, tiled=True),
-        lax.all_gather(shards[1], "fsdp", axis=0, tiled=True),
-        lax.all_gather(shards[2], "fsdp", axis=0, tiled=True),
-        lax.all_gather(shards[3], "fsdp", axis=0, tiled=True),
-        lax.all_gather(shards[4], "fsdp", axis=0, tiled=True),
-        lax.all_gather(shards[5], "fsdp", axis=0, tiled=True),
-        lax.all_gather(shards[6], "fsdp", axis=0, tiled=True),
-        lax.all_gather(shards[7], "fsdp", axis=0, tiled=True),
-        lax.all_gather(shards[8], "fsdp", axis=0, tiled=True),
-        lax.all_gather(shards[9], "fsdp", axis=0, tiled=True),
-        lax.all_gather(shards[10], "fsdp", axis=0, tiled=True),
-        lax.all_gather(shards[11], "fsdp", axis=0, tiled=True),
-        lax.all_gather(shards[12], "fsdp", axis=0, tiled=True),
-        lax.all_gather(shards[13], "fsdp", axis=0, tiled=True),
-        lax.all_gather(shards[14], "fsdp", axis=0, tiled=True),
-    )
-    states = run_layer(tokens, params, segment_ids)
     flat_tokens, query_states, key_states, value_states, joined, log_total = states[:6]
     resid_one, hidden, expanded, active, resid_two = states[6:11]
     w_query_full, w_key_full, w_value_full, w_out_full, w_up_full, w_down_full = params[:6]
@@ -363,40 +360,7 @@
         grad_second_gain,
         grad_second_shift,
     )
-    shares = (
-        lax.psum_scatter(grad_params[0], "fsdp", scatter_dimension=0, tiled=True),
-        lax.psum_scatter(grad_params[1], "fsdp", scatter_dimension=0, tiled=True),
-        lax.psum_scatter(grad_params[2], "fsdp", scatter_dimension=0, tiled=True),
-        lax.psum_scatter(grad_params[3], "fsdp", scatter_dimension=0, tiled=True),
-        lax.psum_scatter(grad_params[4], "fsdp", scatter_dimension=0, tiled=True),
-        lax.psum_scatter(grad_params[5], "fsdp", scatter_dimension=0, tiled=True),
-        lax.psum_scatter(grad_params[6], "fsdp", scatter_dimension=0, tiled=True),
-        lax.psum_scatter(grad_params[7], "fsdp", scatter_dimension=0, tiled=True),
-        lax.psum_scatter(grad_params[8], "fsdp", scatter_dimension=0, tiled=True),
-        lax.psum_scatter(grad_params[9], "fsdp", scatter_dimension=0, tiled=True),
-        lax.psum_scatter(grad_params[10], "fsdp", scatter_dimension=0, tiled=True),
-        lax.psum_scatter(grad_params[11], "fsdp", scatter_dimension=0, tiled=True),
-        lax.psum_scatter(grad_params[12], "fsdp", scatter_dimension=0, tiled=True),
-        lax.psum_scatter(grad_params[13], "fsdp", scatter_dimension=0, tiled=True),
-        lax.psum_scatter(grad_params[14], "fsdp", scatter_dimension=0, tiled=True),
-    )
-    totals = (
-        lax.psum(shares[0].astype(jnp.bfloat16), "rep").astype(jnp.float32),
-        lax.psum(shares[1].astype(jnp.bfloat16), "rep").astype(jnp.float32),
-        lax.psum(shares[2].astype(jnp.bfloat16), "rep").astype(jnp.float32),
-        lax.psum(shares[3].astype(jnp.bfloat16), "rep").astype(jnp.float32),
-        lax.psum(shares[4].astype(jnp.bfloat16), "rep").astype(jnp.float32),
-        lax.psum(shares[5].astype(jnp.bfloat16), "rep").astype(jnp.float32),
-        lax.psum(shares[6].astype(jnp.bfloat16), "rep").astype(jnp.float32),
-        lax.psum(shares[7].astype(jnp.bfloat16), "rep").astype(jnp.float32),
-        lax.psum(shares[8].astype(jnp.bfloat16), "rep").astype(jnp.float32),
-        lax.psum(shares[9].astype(jnp.bfloat16), "rep").astype(jnp.float32),
-        lax.psum(shares[10].astype(jnp.bfloat16), "rep").astype(jnp.float32),
-        lax.psum(shares[11].astype(jnp.bfloat16), "rep").astype(jnp.float32),
-        lax.psum(shares[12].astype(jnp.bfloat16), "rep").astype(jnp.float32),
-        lax.psum(shares[13].astype(jnp.bfloat16), "rep").astype(jnp.float32),
-        lax.psum(shares[14].astype(jnp.bfloat16), "rep").astype(jnp.float32),
-    )
+    totals = reduce_all(grad_params)
     return (
         output.astype(jnp.bfloat16),
         grad_inputs.reshape(row_shape).astype(jnp.bfloat16),

time: 924 us -> 900 us (0.974)
  local copies, waits for them, and re-layouts: 115 us -> 223 us
  matrix products: 277 us -> 188 us
  blocking collectives: 117 us -> 45.5 us
  waiting for transfers between devices: 333 us -> 383 us
  other arithmetic: 58.7 us -> 37.8 us
    reduce_scatter x4 -> x0, waiting for transfers between devices: 198 us -> none  [the longest x1 78.1 us: local(): lax.psum_scatter(grad_params[4], 'fsdp', scatter_dimension=0, tiled=True)]
    all_gather x6 -> x1, waiting for transfers between devices: 15.7 us -> 138 us  [gather_all(): gathered = lax.all_gather(packed, 'fsdp', axis=0, tiled=True)]
    unnamed x17 -> x4, waiting for transfers between devices: 87.4 us -> 185 us
    reshape x0 -> x30, local copies, waits for them, and re-layouts: none -> 84.1 us  [the longest x1 31.3 us: reduce_all(): packed.reshape(-1)]
    dot_general x8 -> x5, matrix products: 107 us -> 50.5 us  [project(): jnp.dot(inputs, weight, preferred_element_type=jnp.float32)]
    unnamed x2 -> x0, blocking collectives: 50.5 us -> none
    unnamed x208 -> x197, local copies, waits for them, and re-layouts: 45.1 us -> 74.8 us
    psum x1, waiting for transfers between devices: 31.6 us -> 59.4 us  [reduce_all(): total = lax.psum(share, 'rep').astype(jnp.float32)]
  transfers between devices with their start and end apart: 14 -> 3, of which waited for: 7 -> 3; matrix products, arithmetic and copies ran while one was open for 38% -> 2% of each run, Pallas kernels for 0% -> 0%
where the time goes in v1:
time: 900 us; the launch traced here: 894 us
  waiting for transfers between devices  383 us (43%)
  local copies, waits for them, and re-layouts  223 us (25%)
  matrix products  188 us (21%)
  blocking collectives  45.5 us (5%)
  other arithmetic  37.8 us (4%)
  between operations  15.7 us (2%)
    unnamed x4, waiting for transfers between devices  185 us
    all_gather x1, waiting for transfers between devices, gather_all(): gathered = lax.all_gather(packed, 'fsdp', axis=0, tiled=True)  138 us
    unnamed x197, local copies, waits for them, and re-layouts  74.8 us
    psum x1, waiting for transfers between devices, reduce_all(): total = lax.psum(share, 'rep').astype(jnp.float32)  59.4 us
    dot_general x5, matrix products, project(): jnp.dot(inputs, weight, preferred_element_type=jnp.float32)  50.5 us
    all_gather x1, blocking collectives, local(): lax.all_gather(local_embed, ('rep', 'fsdp'), axis=0, tiled=True)  45.5 us
    reshape x1, local copies, waits for them, and re-layouts, reduce_all(): packed.reshape(-1)  31.3 us
    reshape x11, local copies, waits for them, and re-layouts, reduce_all(): piece.astype(jnp.bfloat16).reshape(group, -1)  22.6 us
  transfers between devices with their start and end apart: 3, of which 3 were waited for; matrix products, arithmetic and copies ran while one was open for 2% of the time, Pallas kernels for 0%

profile of v1, /device:TPU:0, one launch (start us, length us, event | category | flops | bytes accessed | tf_op | source)
XLA Modules:
  0.0 893.9 jit_solution(13313679677062686084)
XLA Ops:
  13.5 8.3 concatenate.6
  21.8 21.0 %reshape.604 = bf16[1,1,885888]{2,1,0:T(2,128)(2,1)} reshape(bf16[885888]{0:T(1024)(128)(2,1)S(1)} %concatenate.6) | data formatting | bytes 3543552
  46.1 138.4 %all-gather.3.cloned.1.call-done = bf16[8,1,885888]{2,1,0:T(2,128)(2,1)} async-done(((bf16[1,1,885888]{2,1,0:T(2,128)(2,1)}), bf16[8,1,885888]{2,1,0:T(2,128)(2,1)}) %all-gather.3.cloned.1.call-update) | async-done | bytes 14174224 | tf_op jit(solution)/shard_map/all_gather | solution.py:164
  184.5 13.1 %copy.121 = bf16[8,1,885888]{2,0,1:T(8,128)(2,1)S(1)} copy(bf16[8,1,885888]{2,1,0:T(2,128)(2,1)} %all-gather.3.cloned.1.call-done) | data formatting | bytes 28348416
  216.6 24.3 %while.26 = (s32[]{:T(128)}, bf16[2,512,768]{2,1,0:T(8,128)(2,1)}, f32[2,12,512,1]{2,1,3,0:T(8,128)}, bf16[2,512,768]{1,2,0:T(8,128)(2,1)S(1)}, s32[2,512]{1,0:T...) while((s32[]{:T(128)}, bf16[2,512,768]{2,1,0:T(8,128)(2,1)}, ...), condition=%wide.region_3.4_spmd, body=%wide.region_0.3_spmd.sunk | while | flops 843704320 | bytes 50019424 | solution.py:128
  249.6 6.6 reshape.550
  256.3 6.9 reshape.551
  263.2 38.1 %multiply_convert_fusion.3 = (bf16[1024,3072]{1,0:T(8,128)(2,1)S(1)}, f32[1024,3072]{1,0:T(8,128)}, f32[1024,3072]{1,0:T(8,128)}) fusion(f32[3072]{0:T(1024)S(1)} %reshape.582, bf16[768,3072]{1,0:T(8,128)(2,1)} %reshape.550, f32[1024,768]{1,0:T(8,128)S(1)} %copy-done.6, f32[768]{0:T(1024)S(1)} %reshape.581, f32[768]{0:T(1024)S(1)} %reshape.580, ...), kind=kOutput, calls=%fused_computation.43 | convolution fusion | flops 5043388416 | bytes 39348224 | tf_op jit(solution)/shard_map/dot_general | solution.py:31
  311.2 45.5 %all_gather.7 = bf16[512,768]{1,0:T(8,128)(2,1)} all-gather(bf16[16,768]{1,0:T(8,128)(2,1)S(1)} %fusion.38), channel_id=1, replica_groups=mesh['rep'=4,'fsdp'=8] {'rep','fsdp'}, dimensions={0}, use_global_device_ids=true | all-gather | bytes 811008 | tf_op jit(solution)/shard_map/all_gather | solution.py:238
  379.8 17.6 %fusion.80 = (bf16[3072]{0:T(1024)(128)(2,1)}, bf16[1024,3072]{1,0:T(8,128)(2,1)}) fusion(f32[1024,3072]{1,0:T(8,128)} %get-tuple-element.230, bf16[1024,768]{1,0:T(8,128)(2,1)S(1)} %get-tuple-element.222, bf16[3072,768]{1,0:T(8,128)(2,1)} %reshape.551, f32[1024,3072]{1,0:T(8,128)} %get-tuple-element.269, f32[3072]{0:T(1024)S(1)} %copy-done.66), kind=kOutput, calls=%fused_computation.192 | convolution fusion | flops 4882166784 | bytes 37767168 | tf_op jit(solution)/shard_map/nd,fd->nf/dot_general | solution.py:288
  397.4 10.1 %convolution_convert_fusion.1 = bf16[768,3072]{1,0:T(8,128)(2,1)} fusion(bf16[1024,3072]{1,0:T(8,128)(2,1)} %get-tuple-element.282, f32[1024,768]{1,0:T(8,128)S(1)} %copy-done.8, f32[768]{0:T(1024)S(1)} %copy-done.78, f32[768]{0:T(1024)S(1)} %copy-done.58, f32[1024]{0:T(1024)S(1)} %copy-done.56, f32[1024]{0:T(1024)S(1)} %copy-done.50), kind=kOutput, calls=%fused_computation.58 | convolution fusion | flops 4838129664 | bytes 14170112 | tf_op jit(solution)/shard_map/nd,nf->df/dot_general | solution.py:293
  407.6 9.0 %multiply_reduce_fusion.1 = (bf16[768]{0:T(1024)(128)(2,1)}, f32[1024]{0:T(1024)S(1)}, bf16[768]{0:T(1024)(128)(2,1)}, f32[1024,768]{1,0:T(8,128)S(1)}) fusion(f32[1024,768]{1,0:T(8,128)S(1)} %copy-done.8, f32[1024]{0:T(1024)S(1)} %copy-done.56, f32[1024]{0:T(1024)S(1)} %copy-done.50, f32[768]{0:T(1024)S(1)} %copy-done.58, ...), kind=kOutput, calls=%fused_computation.64 | convolution fusion | flops 4839699456 | bytes 20469760 | tf_op jit(solution)/shard_map/nf,df->nd/dot_general | solution.py:297
  425.5 7.2 convolution_convert_fusion
  432.7 79.2 %while.27 = (s32[]{:T(128)}, bf16[2,512,768]{1,2,0:T(8,128)(2,1)}, bf16[2,512,768]{1,2,0:T(8,128)(2,1)}, bf16[2,512,768]{1,2,0:T(8,128)(2,1)}, bf16[2,512,768]{1...) while((s32[]{:T(128)}, bf16[2,512,768]{1,2,0:T(8,128)(2,1)}, ...), condition=%wide.region_22.23_spmd, body=%wide.region_20.22_spmd.sunk | while | flops 2062673920 | bytes 185252720 | solution.py:311
  443.3 11.0 %multiply_reduce_fusion.9 = (f32[12,512]{1,0:T(8,128)S(1)}, f32[12,512,512]{1,2,0:T(8,128)}) fusion(f32[12,512,512]{1,2,0:T(8,128)} %fusion.174, f32[12,512]{1,0:T(8,128)S(1)} %dynamic-slice_bitcast_fusion.2, pred[512,512]{0,1:T(8,128)(4,1)S(1)} %broadcast_compare_fusion.5, bf16[512,12,64]{0,2,1:T(8,128)(2,1)S(1)} %bitcast.201, ...), kind=kOutput, calls=%fused_computation.19.clone.1 | convolution fusion | flops 418375680 | bytes 27049984 | tf_op jit(solution)/shard_map/while/body/eval_jaxpr/qhd,khd->hqk/dot_general | solution.py:73
  455.9 6.9 multiply_convert_fusion.8
  474.5 6.4 fusion.174
  482.7 11.0 %multiply_reduce_fusion.9 = (f32[12,512]{1,0:T(8,128)S(1)}, f32[12,512,512]{1,2,0:T(8,128)}) fusion(f32[12,512,512]{1,2,0:T(8,128)} %fusion.174, f32[12,512]{1,0:T(8,128)S(1)} %dynamic-slice_bitcast_fusion.2, pred[512,512]{0,1:T(8,128)(4,1)S(1)} %broadcast_compare_fusion.5, bf16[512,12,64]{0,2,1:T(8,128)(2,1)S(1)} %bitcast.201, ...), kind=kOutput, calls=%fused_computation.19.clone.1 | convolution fusion | flops 418375680 | bytes 27049984 | tf_op jit(solution)/shard_map/while/body/eval_jaxpr/qhd,khd->hqk/dot_general | solution.py:73
  495.3 6.9 multiply_convert_fusion.8
  519.3 6.6 reshape.563
  546.0 6.6 reshape.564
  578.4 31.3 %reshape.570 = bf16[7087104]{0:T(1024)(128)(2,1)} reshape(bf16[8,885888]{1,0:T(8,128)(2,1)} %dynamic-update-slice.14) | data formatting | bytes 28348416 | tf_op jit(solution)/shard_map/reshape | solution.py:179
  611.6 184.8 %all-reduce.6.cloned.1.call-done = bf16[7087104]{0:T(1024)(128)(2,1)} async-done(((bf16[7087104]{0:T(1024)(128)(2,1)}), bf16[7087104]{0:T(1024)(128)(2,1)}) %all-reduce.6.cloned.1.call-update) | async-done | bytes 14174224
  817.0 59.4 %all-reduce.4.cloned.1.call-done = bf16[885888]{0:T(1024)(128)(2,1)} async-done(((bf16[885888]{0:T(1024)(128)(2,1)}), bf16[885888]{0:T(1024)(128)(2,1)}) %all-reduce.4.cloned.1.call-update) | async-done | bytes 1771792 | tf_op jit(solution)/shard_map/psum | solution.py:180
  (398 shorter events, 224.3 us)
Async XLA Ops:
  7.2 177.3 %all-gather.3.cloned.1.call-start = ((), (), s32[]{:S(2)}) async-start(), calls=%async_computation.1 | async-start | bytes 31891968 | tf_op jit(solution)/shard_map/all_gather | solution.py:164
  21.8 21.3 %copy-start.75 = (s32[512]{0:T(512)S(1)}, s32[512]{0:T(512)}, u32[]{:S(2)}) copy-start(s32[512]{0:T(512)} %param.24) | copy-start | bytes 6148
  21.8 22.4 %copy-start.36 = (s32[2,512]{1,0:T(2,128)S(1)}, s32[2,512]{1,0:T(2,128)}, u32[]{:S(2)}) copy-start(s32[2,512]{1,0:T(2,128)} %param.23) | copy-start | bytes 12292
  42.9 753.5 %all-reduce.6.cloned.1.call-start = ((), (), s32[]{:S(2)}) async-start(), calls=%async_computation.2 | async-start | bytes 28348416
  216.6 24.3 %copy-start.64 = (f32[8,96]{1,0:T(8,128)S(1)}, f32[8,96]{1,0:T(8,128)}, u32[]{:S(2)}) copy-start(f32[8,96]{1,0:T(8,128)} %get-tuple-element.244) | copy-start | bytes 9220
  247.2 54.1 %copy-start.49 = (f32[1024]{0:T(1024)}, f32[1024]{0:T(1024)S(1)}, u32[]{:S(2)}) copy-start(f32[1024]{0:T(1024)S(1)} %broadcast_multiply_fusion.1) | copy-start | bytes 12292
  249.4 51.9 %copy-start.55 = (f32[1024]{0:T(1024)}, f32[1024]{0:T(1024)S(1)}, u32[]{:S(2)}) copy-start(f32[1024]{0:T(1024)S(1)} %fusion.58) | copy-start | bytes 12292
  249.5 51.8 %copy-start.57 = (f32[768]{0:T(1024)}, f32[768]{0:T(1024)S(1)}, u32[]{:S(2)}) copy-start(f32[768]{0:T(1024)S(1)} %reshape.580) | copy-start | bytes 9220
  249.6 51.8 %copy-start.77 = (f32[768]{0:T(1024)}, f32[768]{0:T(1024)S(1)}, u32[]{:S(2)}) copy-start(f32[768]{0:T(1024)S(1)} %reshape.581) | copy-start | bytes 9220
  263.1 38.2 %copy-start.7 = (f32[1024,768]{1,0:T(8,128)S(1)}, f32[1024,768]{1,0:T(8,128)}, u32[]{:S(2)}) copy-start(f32[1024,768]{1,0:T(8,128)} %copy-done.5) | copy-start | bytes 9437188
  263.2 38.2 %copy-start.22 = (bf16[3072,768]{1,0:T(8,128)(2,1)S(1)}, bf16[3072,768]{1,0:T(8,128)(2,1)}, u32[]{:S(2)}) copy-start(bf16[3072,768]{1,0:T(8,128)(2,1)} %reshape.551) | copy-start | bytes 14155780
  306.8 69.3 %copy-start = (f32[1024,768]{1,0:T(8,128)}, f32[1024,768]{1,0:T(8,128)S(1)}, u32[]{:S(2)}) copy-start(f32[1024,768]{1,0:T(8,128)S(1)} %get-tuple-element.271) | copy-start | bytes 9437188
  306.9 69.2 %copy-start.38 = (f32[1024]{0:T(1024)}, f32[1024]{0:T(1024)S(1)}, u32[]{:S(2)}) copy-start(f32[1024]{0:T(1024)S(1)} %broadcast_multiply_fusion) | copy-start | bytes 12292
  307.4 68.7 %copy-start.40 = (f32[1024]{0:T(1024)}, f32[1024]{0:T(1024)S(1)}, u32[]{:S(2)}) copy-start(f32[1024]{0:T(1024)S(1)} %fusion.59) | copy-start | bytes 12292
  307.9 68.2 %copy-start.42 = (f32[768]{0:T(1024)}, f32[768]{0:T(1024)S(1)}, u32[]{:S(2)}) copy-start(f32[768]{0:T(1024)S(1)} %reshape.584) | copy-start | bytes 9220
  309.9 50.3 %copy-start.69 = (f32[2,8]{1,0:T(2,128)}, f32[2,8]{1,0:T(2,128)S(1)}, u32[]{:S(2)}) copy-start(f32[2,8]{1,0:T(2,128)S(1)} %get-tuple-element.272) | copy-start | bytes 196
  309.9 50.3 %copy-start.68 = (f32[2,8]{1,0:T(2,128)}, f32[2,8]{1,0:T(2,128)S(1)}, u32[]{:S(2)}) copy-start(f32[2,8]{1,0:T(2,128)S(1)} %add_rsqrt_fusion) | copy-start | bytes 196
  379.8 17.6 %copy-start.8 = (f32[1024,768]{1,0:T(8,128)S(1)}, f32[1024,768]{1,0:T(8,128)}, u32[]{:S(2)}) copy-start(f32[1024,768]{1,0:T(8,128)} %copy-done.5) | copy-start | bytes 9437188
  379.8 17.6 %copy-start.50 = (f32[1024]{0:T(1024)S(1)}, f32[1024]{0:T(1024)}, u32[]{:S(2)}) copy-start(f32[1024]{0:T(1024)} %copy-done.49) | copy-start | bytes 12292
  379.8 17.6 %copy-start.56 = (f32[1024]{0:T(1024)S(1)}, f32[1024]{0:T(1024)}, u32[]{:S(2)}) copy-start(f32[1024]{0:T(1024)} %copy-done.55) | copy-start | bytes 12292
  379.8 17.6 %copy-start.58 = (f32[768]{0:T(1024)S(1)}, f32[768]{0:T(1024)}, u32[]{:S(2)}) copy-start(f32[768]{0:T(1024)} %copy-done.57) | copy-start | bytes 9220
  379.8 17.6 %copy-start.78 = (f32[768]{0:T(1024)S(1)}, f32[768]{0:T(1024)}, u32[]{:S(2)}) copy-start(f32[768]{0:T(1024)} %copy-done.77) | copy-start | bytes 9220
  482.7 12.6 %slice-start.2 = ((s8[12582912]{0:T(1024)(128)(4,1)}), s8[4194304]{0:T(1024)(128)(4,1)S(1)}, s32[]{:S(2)}) async-start(s8[12582912]{0:T(1024)(128)(4,1)} %bitcast.194), calls=%async_computation.5 | async-start | bytes 8388608 | tf_op jit(solution)/shard_map/while
  609.7 266.7 %all-reduce.4.cloned.1.call-start = ((), (), s32[]{:S(2)}) async-start(), calls=%async_computation | async-start | bytes 3547136 | tf_op jit(solution)/shard_map/psum | solution.py:180
  (84 other events, 378.4 us)
Sparse Core Ops, SparseCore 0:
  43.0 141.5 all-gather.2
  609.8 186.4 all-reduce.5
  800.2 76.2 all-reduce.3
